TPU v7x, 512 devices: a whole 4x8x8 slice. The times are simulated.
512 devices in a mesh: dp: 8 (over z), expert: 64 (over x, y, core).
Axes of the slice: x: 4, y: 8, z: 8, core: 2. Of those that a mesh axis runs over, the one named last changes fastest.
Arguments:
- tokens: bfloat16 [65536, 1024], P(('dp', 'expert')), may hold values from -6 to 6
- cotangent: bfloat16 [65536, 1024], P(('dp', 'expert')), may hold values from -6 to 6
- routes: int32 [65536, 8], P(('dp', 'expert')), may hold values from 0 to 63, as said below
- combine: float32 [65536, 8], P(('dp', 'expert')), may hold values from 0.1 to 0.5
- w_gate: bfloat16 [64, 1024, 384], P('expert', 'dp'), may hold values from -0.1875 to 0.1875
- w_up: bfloat16 [64, 1024, 384], P('expert', 'dp'), may hold values from -0.1875 to 0.1875
- w_down: bfloat16 [64, 384, 1024], P('expert', None, 'dp'), may hold values from -0.3125 to 0.3125
Outputs:
- mixed: bfloat16 [65536, 1024], P(('dp', 'expert'))
- input_grad: bfloat16 [65536, 1024], P(('dp', 'expert'))
- combine_grad: float32 [65536, 8], P(('dp', 'expert'))
Inputs may be any that keep to these rules, and one draw needn't show every extreme that they name: `routes`: each row names 8 different experts. Among the rows of one device (aligned blocks of 128 rows) each of 2 frequent experts, the same ones on every device, is named by 48 to 56 rows, and every other expert by at most 15 rows, with the counts of the other experts on one device differing by at most one. In every draw some device has a frequent expert named by exactly 56 rows and some device an other expert named by exactly 15 rows.
All inputs are finite; a program needn't handle non-finite values.
Results may differ from a plain program's by a relative error of at most 0.017.
Values may be sent and summed in bfloat16 or wider, within the bound.
No kernel may reach another device: no remote copies, remote signals or barrier semaphores. Data moves between devices by JAX's collectives and lax.ppermute only.
A program may use at most 128 MiB of HBM per device.

v0:
```python
import jax
import jax.numpy as jnp
from jax import lax
from jax.sharding import PartitionSpec as P

HOT = 2


def broadcast(block, axis, owner):
    block = jnp.where(lax.axis_index(axis) == owner, block, jnp.zeros_like(block))
    return lax.psum(block, axis)


def to_owner(array, owners, local_count):
    shape = array.shape
    grouped = array.reshape((owners, local_count) + shape[1:])
    grouped = jnp.swapaxes(grouped, 0, 1)
    return grouped.reshape((local_count, owners * shape[1]) + shape[2:])


def from_owner(array, owners, local_count):
    shape = array.shape
    grouped = array.reshape((local_count, owners, shape[1] // owners) + shape[2:])
    grouped = jnp.swapaxes(grouped, 0, 1)
    return grouped.reshape((owners * local_count, shape[1] // owners) + shape[2:])


def expert_block(row_x, row_dy, row_g, w_g, w_u, w_d):
    gate_pre = jnp.einsum("erd,edf->erf", row_x, w_g, preferred_element_type=jnp.float32)
    up_proj = jnp.einsum("erd,edf->erf", row_x, w_u, preferred_element_type=jnp.float32)
    sigmoid_val = jax.nn.sigmoid(gate_pre)
    silu_val = gate_pre * sigmoid_val
    hidden = (silu_val * up_proj).astype(jnp.bfloat16)
    expert_out = jnp.einsum("erf,efd->erd", hidden, w_d, preferred_element_type=jnp.float32).astype(
        jnp.bfloat16
    )
    dot_grad = jnp.einsum("erd,efd->erf", row_dy, w_d, preferred_element_type=jnp.float32)
    hidden_grad = row_g[:, :, None] * dot_grad
    gate_grad = (
        hidden_grad * up_proj * sigmoid_val * (1.0 + gate_pre * (1.0 - sigmoid_val))
    ).astype(jnp.bfloat16)
    up_grad = (hidden_grad * silu_val).astype(jnp.bfloat16)
    row_grad = jnp.einsum("erf,edf->erd", gate_grad, w_g, preferred_element_type=jnp.float32)
    row_grad = (
        row_grad + jnp.einsum("erf,edf->erd", up_grad, w_u, preferred_element_type=jnp.float32)
    ).astype(jnp.bfloat16)
    return (expert_out, row_grad)


def on_device(tokens, cotangent, routes, combine, w_gate, w_up, w_down):
    tok_rows, width = tokens.shape
    topk = routes.shape[1]
    owners = lax.axis_size("expert")
    local_count = w_gate.shape[0]
    experts = local_count * owners
    pairs = tok_rows * topk
    hot_most = min(tok_rows, 7 * pairs // (2 * experts))
    hot_least = min(tok_rows * 3 // 4, 3 * pairs // experts)
    capacity = (pairs - HOT * hot_least + experts - HOT - 1) // (experts - HOT)
    cold_rows = experts * capacity
    pool_rows = cold_rows + HOT * hot_most
    expert_ids = routes.reshape(-1)
    one_hot = (expert_ids[:, None] == jnp.arange(experts, dtype=jnp.int32)[None, :]).astype(
        jnp.int32
    )
    rank_in = jnp.sum((jnp.cumsum(one_hot, axis=0) - 1) * one_hot, axis=1)
    counts = jnp.sum(one_hot, axis=0)
    top_counts, top_ids = lax.top_k(counts, HOT)
    hot_list = jnp.sort(top_ids)
    match = expert_ids[:, None] == hot_list[None, :]
    is_hot = jnp.any(match, axis=1)
    hot_rank = (
        jnp.sum(jnp.where(match, jnp.arange(HOT, dtype=jnp.int32)[None, :] * hot_most, 0), axis=1)
        + rank_in
    )
    slot_index = jnp.where(is_hot, cold_rows + hot_rank, expert_ids * capacity + rank_in)
    token_index = jnp.arange(pairs, dtype=jnp.int32) // topk
    source_token = jnp.full((pool_rows,), tok_rows, jnp.int32).at[slot_index].set(token_index)
    source_pair = (
        jnp.full((pool_rows,), pairs, jnp.int32)
        .at[slot_index]
        .set(jnp.arange(pairs, dtype=jnp.int32))
    )
    pool_x = jnp.take(tokens, source_token, axis=0, mode="fill", fill_value=0)
    pool_dy = jnp.take(cotangent, source_token, axis=0, mode="fill", fill_value=0)
    pool_g = jnp.take(combine.reshape(-1), source_pair, axis=0, mode="fill", fill_value=0)
    send_x = pool_x[:cold_rows].reshape(experts, capacity, width)
    send_dy = pool_dy[:cold_rows].reshape(experts, capacity, width)
    send_g = pool_g[:cold_rows].reshape(experts, capacity)
    hot_x = pool_x[cold_rows:].reshape(HOT, hot_most, width)
    hot_dy = pool_dy[cold_rows:].reshape(HOT, hot_most, width)
    hot_g = pool_g[cold_rows:].reshape(HOT, hot_most)
    recv_x, recv_dy, recv_g = (
        lax.all_to_all(send_x, "expert", split_axis=0, concat_axis=0, tiled=True),
        lax.all_to_all(send_dy, "expert", split_axis=0, concat_axis=0, tiled=True),
        lax.all_to_all(
            send_g.astype(jnp.bfloat16), "expert", split_axis=0, concat_axis=0, tiled=True
        ).astype(send_g.dtype),
    )
    full_gate, full_up, full_down = (
        lax.all_gather(w_gate, "dp", axis=1, tiled=True),
        lax.all_gather(w_up, "dp", axis=1, tiled=True),
        lax.all_gather(w_down, "dp", axis=2, tiled=True),
    )
    gate_list = []
    up_list = []
    down_list = []
    for which in range(HOT):
        root = hot_list[which] // local_count
        local_slot = hot_list[which] % local_count
        piece_gate = lax.dynamic_index_in_dim(w_gate, local_slot, 0, keepdims=False)
        piece_up = lax.dynamic_index_in_dim(w_up, local_slot, 0, keepdims=False)
        piece_down = lax.dynamic_index_in_dim(w_down, local_slot, 0, keepdims=False)
        shard_gate, shard_up, shard_down = (
            broadcast(piece_gate, "expert", root),
            broadcast(piece_up, "expert", root),
            broadcast(piece_down, "expert", root),
        )
        got_gate, got_up, got_down = (
            lax.all_gather(shard_gate, "dp", axis=0, tiled=True),
            lax.all_gather(shard_up, "dp", axis=0, tiled=True),
            lax.all_gather(shard_down, "dp", axis=1, tiled=True),
        )
        gate_list.append(got_gate)
        up_list.append(got_up)
        down_list.append(got_down)
    hot_out, hot_grad = expert_block(
        hot_x, hot_dy, hot_g, jnp.stack(gate_list), jnp.stack(up_list), jnp.stack(down_list)
    )
    row_x = to_owner(recv_x, owners, local_count)
    row_dy = to_owner(recv_dy, owners, local_count)
    row_g = to_owner(recv_g, owners, local_count)
    expert_out, row_grad = expert_block(row_x, row_dy, row_g, full_gate, full_up, full_down)
    back_out, back_grad = (
        lax.all_to_all(
            from_owner(expert_out, owners, local_count),
            "expert",
            split_axis=0,
            concat_axis=0,
            tiled=True,
        ),
        lax.all_to_all(
            from_owner(row_grad, owners, local_count),
            "expert",
            split_axis=0,
            concat_axis=0,
            tiled=True,
        ),
    )
    pool_out = jnp.concatenate(
        [back_out.reshape(cold_rows, width), hot_out.reshape(HOT * hot_most, width)], axis=0
    )
    pool_grad = jnp.concatenate(
        [back_grad.reshape(cold_rows, width), hot_grad.reshape(HOT * hot_most, width)], axis=0
    )
    out_pairs = pool_out[slot_index].reshape(tok_rows, topk, width)
    grad_pairs = pool_grad[slot_index].reshape(tok_rows, topk, width)
    mixed = jnp.einsum("tk,tkd->td", combine, out_pairs.astype(jnp.float32)).astype(jnp.bfloat16)
    input_grad = jnp.sum(grad_pairs.astype(jnp.float32), axis=1).astype(jnp.bfloat16)
    combine_grad = jnp.einsum(
        "tkd,td->tk", out_pairs, cotangent, preferred_element_type=jnp.float32
    )
    return (mixed, input_grad, combine_grad)


def solution(mesh):
    placed = (
        P(("dp", "expert"), None),
        P(("dp", "expert"), None),
        P(("dp", "expert"), None),
        P(("dp", "expert"), None),
        P("expert", "dp", None),
        P("expert", "dp", None),
        P("expert", None, "dp"),
    )
    return jax.shard_map(
        on_device,
        mesh=mesh,
        in_specs=placed,
        out_specs=(P(("dp", "expert"), None), P(("dp", "expert"), None), P(("dp", "expert"), None)),
        check_vma=False,
    )
```

profile of v0, /device:TPU:22, one launch (start us, length us, event | category | flops | bytes accessed | tf_op | source)
XLA Modules:
  0.0 678.3 jit_solution(17495965251228169367)
XLA Ops:
  7.2 0.7 broadcast_multiply_fusion
  7.9 0.8 copy.23
  9.1 0.8 copy.28
  10.0 18.0 %reduce-window.6 = s32[64,8,128]{2,1,0:T(8,128)S(1)} reduce-window(s32[64,8,128]{2,1,0:T(8,128)S(1)} %fusion.22, s32[]{:T(128)} %constant.105.clone.1), window={size=1x1x128 pad=0_0x0_0x127_0}, to_apply=%region_5.6 | reduce-window | flops 8323072 | bytes 524292 | tf_op jit(solution)/shard_map/reduce-window
  28.7 2.0 top_k.11
  30.8 0.6 sort.16
  31.9 4.3 scatter_custom_fusion.1
  36.2 4.4 gather_fusion.1
  40.6 0.8 convert_element_type.86
  41.4 10.6 %all-to-all-start.2 = ((bf16[64,1,15]{2,1,0:T(2,128)(2,1)}), bf16[64,1,15]{2,1,0:T(2,128)(2,1)S(1)}, u32[]{:S(2)}, u32[]{:S(2)}) async-start(bf16[64,1,15]{2,1,0:T(2,128)(2,1)} %convert_element_type.86), calls=%async_computation.2 | async-start | bytes 65536 | tf_op jit(solution)/shard_map/all_to_all | solution.py:96
  52.0 4.3 scatter_custom_fusion
  56.4 4.4 gather_fusion.4
  60.8 4.9 gather_fusion.3
  65.7 3.3 broadcast_select_fusion
  69.1 1.4 copy-done.2
  70.6 1.7 reshape.219
  72.9 10.6 %all-to-all-start = ((bf16[64,15,1024]{2,1,0:T(8,128)(2,1)}), bf16[64,15,1024]{2,1,0:T(8,128)(2,1)}, u32[]{:S(2)}, u32[]{:S(2)}) async-start(bf16[64,15,1024]{2,1,0:T(8,128)(2,1)} %reshape.219), calls=%async_computation | async-start | bytes 4194304 | tf_op jit(solution)/shard_map/all_to_all | solution.py:94
  83.5 1.4 slice.60
  85.0 3.7 reshape.229
  88.7 43.9 %all-to-all-done = bf16[64,15,1024]{2,1,0:T(8,128)(2,1)} async-done(((bf16[64,15,1024]{2,1,0:T(8,128)(2,1)}), bf16[64,15,1024]{2,1,0:T(8,128)(2,1)}, u32[]{:S(2)}, u32[]{:S(2)}) %all-to-all-start) | async-done | bytes 1966112 | tf_op jit(solution)/shard_map/all_to_all | solution.py:94
  132.7 8.0 %all-to-all-start.3 = ((bf16[64,15,1024]{2,1,0:T(8,128)(2,1)}), bf16[64,15,1024]{2,1,0:T(8,128)(2,1)}, u32[]{:S(2)}, u32[]{:S(2)}) async-start(bf16[64,15,1024]{2,1,0:T(8,128)(2,1)} %reshape.229), calls=%async_computation.3 | async-start | bytes 4194304 | tf_op jit(solution)/shard_map/all_to_all | solution.py:95
  140.7 34.4 %all_gather.27 = bf16[1,1024,384]{2,1,0:T(8,128)(2,1)} all-gather(bf16[1,128,384]{2,1,0:T(8,128)(2,1)S(1)} %copy-done.11), channel_id=1, replica_groups=mesh['dp'=8,'expert'=64] {'dp'}, dimensions={1}, use_global_device_ids=true | all-gather | bytes 884736 | tf_op jit(solution)/shard_map/all_gather | solution.py:101
  175.2 26.3 %all_gather.28 = bf16[1,1024,384]{2,1,0:T(8,128)(2,1)S(1)} all-gather(bf16[1,128,384]{2,1,0:T(8,128)(2,1)S(1)} %copy-done.9), channel_id=1, replica_groups=mesh['dp'=8,'expert'=64] {'dp'}, dimensions={1}, use_global_device_ids=true | all-gather | bytes 884736 | tf_op jit(solution)/shard_map/all_gather | solution.py:102
  201.5 27.0 %all_gather.29 = bf16[1,384,1024]{2,1,0:T(8,128)(2,1)} all-gather(bf16[1,384,128]{2,1,0:T(8,128)(2,1)S(1)} %copy-done.10), channel_id=1, replica_groups=mesh['dp'=8,'expert'=64] {'dp'}, dimensions={2}, use_global_device_ids=true | all-gather | bytes 884736 | tf_op jit(solution)/shard_map/all_gather | solution.py:103
  228.5 3.7 reshape.220
  232.2 3.0 fusion.16
  235.3 1.2 fusion.12
  236.5 1.2 copy-done.22
  237.7 2.5 convolution_convert_fusion
  240.2 3.8 reshape_transpose_reshape.8
  244.0 10.4 %all-to-all-start.1 = ((bf16[64,15,1024]{2,1,0:T(8,128)(2,1)}), bf16[64,15,1024]{2,1,0:T(8,128)(2,1)}, u32[]{:S(2)}, u32[]{:S(2)}) async-start(bf16[64,15,1024]{2,1,0:T(8,128)(2,1)} %reshape_transpose_reshape.8), calls=%async_computation.1 | async-start | bytes 4194304 | tf_op jit(solution)/shard_map/all_to_all | solution.py:135
  254.5 1.3 fusion.49
  257.1 0.7 select_bitcast_fusion.3
  257.8 0.7 select_bitcast_fusion.1
  258.5 0.7 select_bitcast_fusion.5
  259.8 1.0 slice.58
  260.9 0.7 mul.111
  261.7 0.9 convert_reduce_fusion.1
  262.7 193.6 %all-reduce.3.cloned.1.call-done = (bf16[384,128]{1,0:T(8,128)(2,1)}, bf16[384,128]{1,0:T(8,128)(2,1)}, bf16[128,384]{1,0:T(8,128)(2,1)}, bf16[128,384]{1,0:T(8,...) async-done(((bf16[384,128]{1,0:T(8,128)(2,1)}, bf16[384,128]{1,0:T(8,128)(2,1)}, bf16[128,384]{1,0:T(8,128)(2,1)}, bf16[128,384]{1,0:T(8,128)(2,1)}, ...) | async-done | bytes 589840 | tf_op jit(solution)/shard_map/psum | solution.py:11
  456.2 30.5 %all_gather.31 = bf16[1024,384]{1,0:T(8,128)(2,1)} all-gather(bf16[128,384]{1,0:T(8,128)(2,1)} %get-tuple-element.17), channel_id=1, replica_groups=mesh['dp'=8,'expert'=64] {'dp'}, dimensions={0}, use_global_device_ids=true | all-gather | bytes 884736 | tf_op jit(solution)/shard_map/all_gather | solution.py:120
  486.7 2.6 reshape.230
  489.4 2.5 convolution_multiply_fusion
  491.9 1.5 fusion.14
  493.4 1.2 add_convert_fusion
  494.6 1.6 reshape_transpose_reshape.9
  496.3 11.2 %all-to-all-start.4 = ((bf16[64,15,1024]{2,1,0:T(8,128)(2,1)}), bf16[64,15,1024]{2,1,0:T(8,128)(2,1)}, u32[]{:S(2)}, u32[]{:S(2)}) async-start(bf16[64,15,1024]{2,1,0:T(8,128)(2,1)} %reshape_transpose_reshape.9), calls=%async_computation.4 | async-start | bytes 4194304 | tf_op jit(solution)/shard_map/all_to_all | solution.py:142
  507.5 26.3 %all_gather.30 = bf16[1024,384]{1,0:T(8,128)(2,1)S(1)} all-gather(bf16[128,384]{1,0:T(8,128)(2,1)S(1)} %copy-done.17), channel_id=1, replica_groups=mesh['dp'=8,'expert'=64] {'dp'}, dimensions={0}, use_global_device_ids=true | all-gather | bytes 884736 | tf_op jit(solution)/shard_map/all_gather | solution.py:120
  534.2 26.2 %all_gather.33 = bf16[1024,384]{1,0:T(8,128)(2,1)S(1)} all-gather(bf16[128,384]{1,0:T(8,128)(2,1)S(1)} %copy-done.16), channel_id=1, replica_groups=mesh['dp'=8,'expert'=64] {'dp'}, dimensions={0}, use_global_device_ids=true | all-gather | bytes 884736 | tf_op jit(solution)/shard_map/all_gather | solution.py:121
  560.4 26.4 %all_gather.32 = bf16[1024,384]{1,0:T(8,128)(2,1)S(1)} all-gather(bf16[128,384]{1,0:T(8,128)(2,1)S(1)} %copy-done.15), channel_id=1, replica_groups=mesh['dp'=8,'expert'=64] {'dp'}, dimensions={0}, use_global_device_ids=true | all-gather | bytes 884736 | tf_op jit(solution)/shard_map/all_gather | solution.py:121
  587.3 26.7 %all_gather.35 = bf16[384,1024]{1,0:T(8,128)(2,1)S(1)} all-gather(bf16[384,128]{1,0:T(8,128)(2,1)S(1)} %copy-done.14), channel_id=1, replica_groups=mesh['dp'=8,'expert'=64] {'dp'}, dimensions={1}, use_global_device_ids=true | all-gather | bytes 884736 | tf_op jit(solution)/shard_map/all_gather | solution.py:122
  614.0 24.3 %all_gather.34 = bf16[384,1024]{1,0:T(8,128)(2,1)S(1)} all-gather(bf16[384,128]{1,0:T(8,128)(2,1)S(1)} %copy-done.13), channel_id=1, replica_groups=mesh['dp'=8,'expert'=64] {'dp'}, dimensions={1}, use_global_device_ids=true | all-gather | bytes 884736 | tf_op jit(solution)/shard_map/all_gather | solution.py:122
  639.3 0.7 fusion.7
  640.0 0.8 fusion.5
  640.8 3.8 reshape.224
  644.6 1.7 pad_maximum_fusion
  646.3 5.4 gather_fusion
  651.7 2.4 fusion.2
  654.2 0.8 copy.39
  654.9 1.3 fusion
  656.2 0.7 copy.33
  656.9 3.7 reshape.231
  660.7 1.7 pad_maximum_fusion.1
  662.4 5.4 gather_fusion.2
  667.8 3.7 bitcast_reduce_fusion
  (90 shorter events, 5.3 us)
Async XLA Ops:
  7.2 49.2 %copy-start = (bf16[128,1024]{1,0:T(8,128)(2,1)S(1)}, bf16[128,1024]{1,0:T(8,128)(2,1)}, u32[]{:S(2)}) copy-start(bf16[128,1024]{1,0:T(8,128)(2,1)} %param.10) | copy-start | bytes 786436
  31.4 0.5 copy-start.19
  41.4 30.9 %all-to-all-start.2 = ((bf16[64,1,15]{2,1,0:T(2,128)(2,1)}), bf16[64,1,15]{2,1,0:T(2,128)(2,1)S(1)}, u32[]{:S(2)}, u32[]{:S(2)}) async-start(bf16[64,1,15]{2,1,0:T(2,128)(2,1)} %convert_element_type.86), calls=%async_computation.2 | async-start | bytes 65536 | tf_op jit(solution)/shard_map/all_to_all | solution.py:96
  56.4 4.4 copy-start.1
  69.1 1.4 copy-start.2
  72.3 11.3 %copy-start.3 = (bf16[1072,1024]{1,0:T(8,128)(2,1)S(1)}, bf16[1072,1024]{1,0:T(8,128)(2,1)}, u32[]{:S(2)}) copy-start(bf16[1072,1024]{1,0:T(8,128)(2,1)} %get-tuple-element.25) | copy-start | bytes 6586372
  72.3 0.6 copy-start.12
  72.9 59.8 %all-to-all-start = ((bf16[64,15,1024]{2,1,0:T(8,128)(2,1)}), bf16[64,15,1024]{2,1,0:T(8,128)(2,1)}, u32[]{:S(2)}, u32[]{:S(2)}) async-start(bf16[64,15,1024]{2,1,0:T(8,128)(2,1)} %reshape.219), calls=%async_computation | async-start | bytes 4194304 | tf_op jit(solution)/shard_map/all_to_all | solution.py:94
  88.7 52.0 %copy-start.11 = (bf16[1,128,384]{2,1,0:T(8,128)(2,1)S(1)}, bf16[1,128,384]{2,1,0:T(8,128)(2,1)}, u32[]{:S(2)}) copy-start(bf16[1,128,384]{2,1,0:T(8,128)(2,1)} %param.13) | copy-start | bytes 294916
  88.7 86.5 %copy-start.9 = (bf16[1,128,384]{2,1,0:T(8,128)(2,1)S(1)}, bf16[1,128,384]{2,1,0:T(8,128)(2,1)}, u32[]{:S(2)}) copy-start(bf16[1,128,384]{2,1,0:T(8,128)(2,1)} %param.14) | copy-start | bytes 294916
  88.7 112.8 %copy-start.10 = (bf16[1,384,128]{2,1,0:T(8,128)(2,1)S(1)}, bf16[1,384,128]{2,1,0:T(8,128)(2,1)}, u32[]{:S(2)}) copy-start(bf16[1,384,128]{2,1,0:T(8,128)(2,1)} %param.15) | copy-start | bytes 294916
  132.7 111.3 %all-to-all-start.3 = ((bf16[64,15,1024]{2,1,0:T(8,128)(2,1)}), bf16[64,15,1024]{2,1,0:T(8,128)(2,1)}, u32[]{:S(2)}, u32[]{:S(2)}) async-start(bf16[64,15,1024]{2,1,0:T(8,128)(2,1)} %reshape.229), calls=%async_computation.3 | async-start | bytes 4194304 | tf_op jit(solution)/shard_map/all_to_all | solution.py:95
  232.2 3.0 copy-start.5
  235.3 1.2 copy-start.20
  235.3 2.4 copy-start.7
  236.5 1.2 copy-start.22
  244.0 252.3 %all-to-all-start.1 = ((bf16[64,15,1024]{2,1,0:T(8,128)(2,1)}), bf16[64,15,1024]{2,1,0:T(8,128)(2,1)}, u32[]{:S(2)}, u32[]{:S(2)}) async-start(bf16[64,15,1024]{2,1,0:T(8,128)(2,1)} %reshape_transpose_reshape.8), calls=%async_computation.1 | async-start | bytes 4194304 | tf_op jit(solution)/shard_map/all_to_all | solution.py:135
  254.4 6.4 copy-start.18
  254.4 201.8 %all-reduce.3.cloned.1.call-start = ((), (), s32[]{:S(2)}) async-start(), calls=%async_computation.5 | async-start | bytes 1179648 | tf_op jit(solution)/shard_map/psum | solution.py:11
  489.3 2.5 copy-start.6
  489.4 2.5 copy-start.21
  489.4 2.5 copy-start.23
  496.3 11.3 %copy-start.17 = (bf16[128,384]{1,0:T(8,128)(2,1)S(1)}, bf16[128,384]{1,0:T(8,128)(2,1)}, u32[]{:S(2)}) copy-start(bf16[128,384]{1,0:T(8,128)(2,1)} %get-tuple-element.18) | copy-start | bytes 294916
  496.3 37.6 %copy-start.8 = (bf16[1024,384]{1,0:T(8,128)(2,1)S(1)}, bf16[1024,384]{1,0:T(8,128)(2,1)}, u32[]{:S(2)}) copy-start(bf16[1024,384]{1,0:T(8,128)(2,1)} %all_gather.31) | copy-start | bytes 2359300
  496.3 160.6 %all-to-all-start.4 = ((bf16[64,15,1024]{2,1,0:T(8,128)(2,1)}), bf16[64,15,1024]{2,1,0:T(8,128)(2,1)}, u32[]{:S(2)}, u32[]{:S(2)}) async-start(bf16[64,15,1024]{2,1,0:T(8,128)(2,1)} %reshape_transpose_reshape.9), calls=%async_computation.4 | async-start | bytes 4194304 | tf_op jit(solution)/shard_map/all_to_all | solution.py:142
  507.5 26.7 %copy-start.16 = (bf16[128,384]{1,0:T(8,128)(2,1)S(1)}, bf16[128,384]{1,0:T(8,128)(2,1)}, u32[]{:S(2)}) copy-start(bf16[128,384]{1,0:T(8,128)(2,1)} %get-tuple-element.15) | copy-start | bytes 294916
  533.8 26.6 %copy-start.15 = (bf16[128,384]{1,0:T(8,128)(2,1)S(1)}, bf16[128,384]{1,0:T(8,128)(2,1)}, u32[]{:S(2)}) copy-start(bf16[128,384]{1,0:T(8,128)(2,1)} %get-tuple-element.16) | copy-start | bytes 294916
  560.4 26.9 %copy-start.14 = (bf16[384,128]{1,0:T(8,128)(2,1)S(1)}, bf16[384,128]{1,0:T(8,128)(2,1)}, u32[]{:S(2)}) copy-start(bf16[384,128]{1,0:T(8,128)(2,1)} %get-tuple-element.13) | copy-start | bytes 294916
  586.8 27.1 %copy-start.13 = (bf16[384,128]{1,0:T(8,128)(2,1)S(1)}, bf16[384,128]{1,0:T(8,128)(2,1)}, u32[]{:S(2)}) copy-start(bf16[384,128]{1,0:T(8,128)(2,1)} %get-tuple-element.14) | copy-start | bytes 294916
  651.7 3.2 copy-start.4
Sparse Core Ops, SparseCore 0:
  259.9 196.3 all-reduce.2
where the time goes:
time: 680 us; the launch traced here: 678 us
  blocking collectives  248 us (36%)
  waiting for transfers between devices  238 us (35%)
  local copies, waits for them, and re-layouts  71.4 us (11%)
  starting transfers between devices  51 us (8%)
  other arithmetic  35.4 us (5%)
  matrix products  19 us (3%)
  between operations  15.9 us (2%)
    psum x1, waiting for transfers between devices, broadcast(): return lax.psum(block, axis)  194 us
    all_gather x2, blocking collectives, on_device(): lax.all_gather(shard_gate, 'dp', axis=0, tiled=True)  56.8 us
    all_gather x2, blocking collectives, on_device(): lax.all_gather(shard_up, 'dp', axis=0, tiled=True)  52.6 us
    all_gather x2, blocking collectives, on_device(): lax.all_gather(shard_down, 'dp', axis=1, tiled=True)  51 us
    all_to_all x1, waiting for transfers between devices, on_device(): lax.all_to_all(send_x, 'expert', split_axis=0, concat_axis=0, tiled=True)  43.9 us
    all_gather x1, blocking collectives, on_device(): lax.all_gather(w_gate, 'dp', axis=1, tiled=True)  34.4 us
    all_gather x1, blocking collectives, on_device(): lax.all_gather(w_down, 'dp', axis=2, tiled=True)  27 us
    all_gather x1, blocking collectives, on_device(): lax.all_gather(w_up, 'dp', axis=1, tiled=True)  26.3 us
  transfers between devices with their start and end apart: 6, of which 2 were waited for; matrix products, arithmetic and copies ran while one was open for 11% of the time, Pallas kernels for 0%

commit v1 on v0

--- a/solution.py
+++ b/solution.py
@@ -6,9 +6,13 @@
 HOT = 2
 
 
+def shape_stocks(s0, row_axis):
+    return jnp.sum(lax.all_gather(s0, row_axis), 0)
+
+
 def broadcast(block, axis, owner):
     block = jnp.where(lax.axis_index(axis) == owner, block, jnp.zeros_like(block))
-    return lax.psum(block, axis)
+    return shape_stocks(block, axis)
 
 
 def to_owner(array, owners, local_count):

time: 680 us -> 725 us (1.066)
  the two profiles are of different devices: /device:TPU:22 before, /device:TPU:4 now
where the time goes in v1:
time: 725 us; the launch traced here: 723 us
  waiting for transfers between devices  257 us (35%)
  blocking collectives  247 us (34%)
  local copies, waits for them, and re-layouts  74.6 us (10%)
  other arithmetic  55.3 us (8%)
  starting transfers between devices  51.6 us (7%)
  matrix products  21.8 us (3%)
  between operations  16 us (2%)
    all_gather x6, waiting for transfers between devices, shape_stocks(): return jnp.sum(lax.all_gather(s0, row_axis), 0)  111 us
    all_to_all x1, waiting for transfers between devices, on_device(): lax.all_to_all(send_x, 'expert', split_axis=0, concat_axis=0, tiled=True)  57.4 us
    all_gather x2, blocking collectives, on_device(): lax.all_gather(shard_gate, 'dp', axis=0, tiled=True)  54.6 us
    all_gather x2, blocking collectives, on_device(): lax.all_gather(shard_down, 'dp', axis=1, tiled=True)  52.5 us
    all_gather x2, blocking collectives, on_device(): lax.all_gather(shard_up, 'dp', axis=0, tiled=True)  52.4 us
    all_to_all x1, waiting for transfers between devices, on_device(): lax.all_to_all(from_owner(row_grad, owners, local_count), 'expert', split...  44.9 us
    all_to_all x1, waiting for transfers between devices, on_device(): lax.all_to_all(from_owner(expert_out, owners, local_count), 'expert', spl...  42.4 us
    all_gather x1, blocking collectives, on_device(): lax.all_gather(w_gate, 'dp', axis=1, tiled=True)  34.3 us
  transfers between devices with their start and end apart: 11, of which 5 were waited for; matrix products, arithmetic and copies ran while one was open for 13% of the time, Pallas kernels for 0%

profile of v1, /device:TPU:4, one launch (start us, length us, event | category | flops | bytes accessed | tf_op | source)
XLA Modules:
  0.0 723.0 jit_solution(3519056120360197153)
XLA Ops:
  7.3 0.9 copy.23
  8.4 18.0 %reduce-window.6 = s32[64,8,128]{2,1,0:T(8,128)S(1)} reduce-window(s32[64,8,128]{2,1,0:T(8,128)S(1)} %fusion.22, s32[]{:T(128)} %constant.111.clone.1), window={size=1x1x128 pad=0_0x0_0x127_0}, to_apply=%region_5.6 | reduce-window | flops 8323072 | bytes 524292 | tf_op jit(solution)/shard_map/reduce-window
  27.1 2.0 top_k.11
  35.9 4.3 scatter_custom_fusion.1
  40.3 4.4 gather_fusion.1
  44.7 0.8 convert_element_type.98
  45.5 10.7 %all-to-all-start.2 = ((bf16[64,1,15]{2,1,0:T(2,128)(2,1)}), bf16[64,1,15]{2,1,0:T(2,128)(2,1)S(1)}, u32[]{:S(2)}, u32[]{:S(2)}) async-start(bf16[64,1,15]{2,1,0:T(2,128)(2,1)} %convert_element_type.98), calls=%async_computation.2 | async-start | bytes 65536 | tf_op jit(solution)/shard_map/all_to_all | solution.py:100
  56.2 4.3 scatter_custom_fusion
  60.6 4.4 gather_fusion.4
  65.0 4.9 gather_fusion.3
  69.9 3.3 broadcast_select_fusion
  73.2 1.3 copy-done.2
  74.7 1.7 reshape.201
  76.4 10.7 %all-to-all-start = ((bf16[64,15,1024]{2,1,0:T(8,128)(2,1)}), bf16[64,15,1024]{2,1,0:T(8,128)(2,1)}, u32[]{:S(2)}, u32[]{:S(2)}) async-start(bf16[64,15,1024]{2,1,0:T(8,128)(2,1)} %reshape.201), calls=%async_computation | async-start | bytes 4194304 | tf_op jit(solution)/shard_map/all_to_all | solution.py:98
  87.1 1.4 slice.60
  88.5 3.7 reshape.211
  92.2 57.4 %all-to-all-done = bf16[64,15,1024]{2,1,0:T(8,128)(2,1)} async-done(((bf16[64,15,1024]{2,1,0:T(8,128)(2,1)}), bf16[64,15,1024]{2,1,0:T(8,128)(2,1)}, u32[]{:S(2)}, u32[]{:S(2)}) %all-to-all-start) | async-done | bytes 1966112 | tf_op jit(solution)/shard_map/all_to_all | solution.py:98
  149.6 9.4 %all-to-all-start.3 = ((bf16[64,15,1024]{2,1,0:T(8,128)(2,1)}), bf16[64,15,1024]{2,1,0:T(8,128)(2,1)}, u32[]{:S(2)}, u32[]{:S(2)}) async-start(bf16[64,15,1024]{2,1,0:T(8,128)(2,1)} %reshape.211), calls=%async_computation.3 | async-start | bytes 4194304 | tf_op jit(solution)/shard_map/all_to_all | solution.py:99
  159.5 34.3 %all_gather.51 = bf16[1,1024,384]{2,1,0:T(8,128)(2,1)} all-gather(bf16[1,128,384]{2,1,0:T(8,128)(2,1)S(1)} %copy-done.10), channel_id=1, replica_groups=mesh['dp'=8,'expert'=64] {'dp'}, dimensions={1}, use_global_device_ids=true | all-gather | bytes 884736 | tf_op jit(solution)/shard_map/all_gather | solution.py:105
  193.8 26.2 %all_gather.52 = bf16[1,1024,384]{2,1,0:T(8,128)(2,1)S(1)} all-gather(bf16[1,128,384]{2,1,0:T(8,128)(2,1)S(1)} %copy-done.11), channel_id=1, replica_groups=mesh['dp'=8,'expert'=64] {'dp'}, dimensions={1}, use_global_device_ids=true | all-gather | bytes 884736 | tf_op jit(solution)/shard_map/all_gather | solution.py:106
  220.0 26.7 %all_gather.53 = bf16[1,384,1024]{2,1,0:T(8,128)(2,1)} all-gather(bf16[1,384,128]{2,1,0:T(8,128)(2,1)S(1)} %copy-done.12), channel_id=1, replica_groups=mesh['dp'=8,'expert'=64] {'dp'}, dimensions={2}, use_global_device_ids=true | all-gather | bytes 884736 | tf_op jit(solution)/shard_map/all_gather | solution.py:107
  246.7 3.8 reshape.202
  250.4 3.0 fusion.16
  253.5 1.2 fusion.12
  254.7 1.2 copy-done.20
  255.9 2.5 convolution_convert_fusion
  258.4 3.7 reshape_transpose_reshape.8
  262.1 11.2 %all-to-all-start.1 = ((bf16[64,15,1024]{2,1,0:T(8,128)(2,1)}), bf16[64,15,1024]{2,1,0:T(8,128)(2,1)}, u32[]{:S(2)}, u32[]{:S(2)}) async-start(bf16[64,15,1024]{2,1,0:T(8,128)(2,1)} %reshape_transpose_reshape.8), calls=%async_computation.1 | async-start | bytes 4194304 | tf_op jit(solution)/shard_map/all_to_all | solution.py:139
  273.6 3.8 reshape.212
  277.3 3.1 convolution_multiply_fusion
  280.5 1.5 fusion.14
  282.0 2.5 add_convert_fusion
  284.5 3.7 reshape_transpose_reshape.9
  288.2 42.4 %all-to-all-done.1 = bf16[64,15,1024]{2,1,0:T(8,128)(2,1)} async-done(((bf16[64,15,1024]{2,1,0:T(8,128)(2,1)}), bf16[64,15,1024]{2,1,0:T(8,128)(2,1)}, u32[]{:S(2)}, u32[]{:S(2)}) %all-to-all-start.1) | async-done | bytes 1966112 | tf_op jit(solution)/shard_map/all_to_all | solution.py:139
  330.6 9.4 %all-to-all-start.4 = ((bf16[64,15,1024]{2,1,0:T(8,128)(2,1)}), bf16[64,15,1024]{2,1,0:T(8,128)(2,1)}, u32[]{:S(2)}, u32[]{:S(2)}) async-start(bf16[64,15,1024]{2,1,0:T(8,128)(2,1)} %reshape_transpose_reshape.9), calls=%async_computation.4 | async-start | bytes 4194304 | tf_op jit(solution)/shard_map/all_to_all | solution.py:146
  340.8 1.6 slice.58
  342.4 0.8 copy.30
  343.2 3.8 reshape.206
  347.0 44.9 %all-to-all-done.4 = bf16[64,15,1024]{2,1,0:T(8,128)(2,1)} async-done(((bf16[64,15,1024]{2,1,0:T(8,128)(2,1)}), bf16[64,15,1024]{2,1,0:T(8,128)(2,1)}, u32[]{:S(2)}, u32[]{:S(2)}) %all-to-all-start.4) | async-done | bytes 1966112 | tf_op jit(solution)/shard_map/all_to_all | solution.py:146
  391.9 3.7 reshape.213
  395.6 3.8 reduce_sum.123
  399.4 3.8 reduce_sum.124
  403.2 4.1 reduce_sum.125
  407.3 27.9 %all-gather.7.cloned.1.call-done = bf16[64,128,384]{2,1,0:T(8,128)(2,1)} async-done(((bf16[1,128,384]{2,1,0:T(8,128)(2,1)}), bf16[64,128,384]{2,1,0:T(8,128)(2,1)}) %all-gather.7.cloned.1.call-update) | async-done | bytes 6291472 | tf_op jit(solution)/shard_map/all_gather | solution.py:10
  435.2 3.8 reduce_sum.120
  439.0 82.7 %all-gather.9.cloned.1.call-done = bf16[64,128,384]{2,1,0:T(8,128)(2,1)} async-done(((bf16[1,128,384]{2,1,0:T(8,128)(2,1)}), bf16[64,128,384]{2,1,0:T(8,128)(2,1)}) %all-gather.9.cloned.1.call-update) | async-done | bytes 6291472 | tf_op jit(solution)/shard_map/all_gather | solution.py:10
  521.7 3.8 reduce_sum.121
  525.5 28.3 %all_gather.57 = bf16[1024,384]{1,0:T(8,128)(2,1)S(1)} all-gather(bf16[128,384]{1,0:T(8,128)(2,1)S(1)} %reduce_sum.121), channel_id=1, replica_groups=mesh['dp'=8,'expert'=64] {'dp'}, dimensions={0}, use_global_device_ids=true | all-gather | bytes 884736 | tf_op jit(solution)/shard_map/all_gather | solution.py:124
  553.8 26.3 %all_gather.55 = bf16[1024,384]{1,0:T(8,128)(2,1)S(1)} all-gather(bf16[128,384]{1,0:T(8,128)(2,1)S(1)} %reduce_sum.120), channel_id=1, replica_groups=mesh['dp'=8,'expert'=64] {'dp'}, dimensions={0}, use_global_device_ids=true | all-gather | bytes 884736 | tf_op jit(solution)/shard_map/all_gather | solution.py:124
  580.1 25.4 %all_gather.65 = bf16[384,1024]{1,0:T(8,128)(2,1)S(1)} all-gather(bf16[384,128]{1,0:T(8,128)(2,1)S(1)} %reduce_sum.125), channel_id=1, replica_groups=mesh['dp'=8,'expert'=64] {'dp'}, dimensions={1}, use_global_device_ids=true | all-gather | bytes 884736 | tf_op jit(solution)/shard_map/all_gather | solution.py:126
  605.5 27.1 %all_gather.63 = bf16[384,1024]{1,0:T(8,128)(2,1)} all-gather(bf16[384,128]{1,0:T(8,128)(2,1)S(1)} %reduce_sum.124), channel_id=1, replica_groups=mesh['dp'=8,'expert'=64] {'dp'}, dimensions={1}, use_global_device_ids=true | all-gather | bytes 884736 | tf_op jit(solution)/shard_map/all_gather | solution.py:126
  632.6 26.3 %all_gather.61 = bf16[1024,384]{1,0:T(8,128)(2,1)S(1)} all-gather(bf16[128,384]{1,0:T(8,128)(2,1)S(1)} %reduce_sum.123), channel_id=1, replica_groups=mesh['dp'=8,'expert'=64] {'dp'}, dimensions={0}, use_global_device_ids=true | all-gather | bytes 884736 | tf_op jit(solution)/shard_map/all_gather | solution.py:125
  658.9 3.8 reduce_sum.122
  662.7 26.1 %all_gather.59 = bf16[1024,384]{1,0:T(8,128)(2,1)S(1)} all-gather(bf16[128,384]{1,0:T(8,128)(2,1)S(1)} %reduce_sum.122), channel_id=1, replica_groups=mesh['dp'=8,'expert'=64] {'dp'}, dimensions={0}, use_global_device_ids=true | all-gather | bytes 884736 | tf_op jit(solution)/shard_map/all_gather | solution.py:125
  688.8 1.3 fusion.8
  692.3 0.7 fusion.7
  693.1 0.8 fusion.5
  693.8 0.8 copy-done.5
  694.8 5.4 gather_fusion
  700.2 3.0 fusion
  703.8 0.8 copy.39
  705.3 1.7 pad_maximum_fusion.1
  707.0 5.4 gather_fusion.2
  712.4 3.7 bitcast_reduce_fusion
  (107 shorter events, 11.9 us)
Async XLA Ops:
  7.2 53.4 %copy-start = (bf16[128,1024]{1,0:T(8,128)(2,1)S(1)}, bf16[128,1024]{1,0:T(8,128)(2,1)}, u32[]{:S(2)}) copy-start(bf16[128,1024]{1,0:T(8,128)(2,1)} %param.10) | copy-start | bytes 786436
  7.2 24.5 %copy-start.11 = (bf16[1,128,384]{2,1,0:T(8,128)(2,1)S(1)}, bf16[1,128,384]{2,1,0:T(8,128)(2,1)}, u32[]{:S(2)}) copy-start(bf16[1,128,384]{2,1,0:T(8,128)(2,1)} %param.14) | copy-start | bytes 294916
  7.2 25.2 %copy-start.12 = (bf16[1,384,128]{2,1,0:T(8,128)(2,1)S(1)}, bf16[1,384,128]{2,1,0:T(8,128)(2,1)}, u32[]{:S(2)}) copy-start(bf16[1,384,128]{2,1,0:T(8,128)(2,1)} %param.15) | copy-start | bytes 294916
  7.2 26.8 %copy-start.10 = (bf16[1,128,384]{2,1,0:T(8,128)(2,1)S(1)}, bf16[1,128,384]{2,1,0:T(8,128)(2,1)}, u32[]{:S(2)}) copy-start(bf16[1,128,384]{2,1,0:T(8,128)(2,1)} %param.13) | copy-start | bytes 294916
  7.2 388.4 %all-gather.13.cloned.1.call-start = ((), (), s32[]{:S(2)}) async-start(), calls=%async_computation.8 | async-start | bytes 6389760 | tf_op jit(solution)/shard_map/all_gather | solution.py:10
  8.3 27.0 %copy-start.17 = (s32[128,8]{0,1:T(8,128)S(1)}, s32[128,8]{0,1:T(8,128)}, u32[]{:S(2)}) copy-start(s32[128,8]{0,1:T(8,128)} %param.11) | copy-start | bytes 12292
  8.3 27.2 %copy-start.16 = (f32[128,8]{0,1:T(8,128)S(1)}, f32[128,8]{0,1:T(8,128)}, u32[]{:S(2)}) copy-start(f32[128,8]{0,1:T(8,128)} %param.12) | copy-start | bytes 12292
  32.4 367.0 %all-gather.15.cloned.1.call-start = ((), (), s32[]{:S(2)}) async-start(), calls=%async_computation.9 | async-start | bytes 6389760 | tf_op jit(solution)/shard_map/all_gather | solution.py:10
  33.2 370.1 %all-gather.17.cloned.1.call-start = ((), (), s32[]{:S(2)}) async-start(), calls=%async_computation.10 | async-start | bytes 6389760 | tf_op jit(solution)/shard_map/all_gather | solution.py:10
  33.9 401.3 %all-gather.7.cloned.1.call-start = ((), (), s32[]{:S(2)}) async-start(), calls=%async_computation.5 | async-start | bytes 6389760 | tf_op jit(solution)/shard_map/all_gather | solution.py:10
  34.7 487.0 %all-gather.9.cloned.1.call-start = ((), (), s32[]{:S(2)}) async-start(), calls=%async_computation.6 | async-start | bytes 6389760 | tf_op jit(solution)/shard_map/all_gather | solution.py:10
  45.5 30.9 %all-to-all-start.2 = ((bf16[64,1,15]{2,1,0:T(2,128)(2,1)}), bf16[64,1,15]{2,1,0:T(2,128)(2,1)S(1)}, u32[]{:S(2)}, u32[]{:S(2)}) async-start(bf16[64,1,15]{2,1,0:T(2,128)(2,1)} %convert_element_type.98), calls=%async_computation.2 | async-start | bytes 65536 | tf_op jit(solution)/shard_map/all_to_all | solution.py:100
  60.6 4.4 copy-start.1
  73.2 1.3 copy-start.2
  76.4 10.7 %copy-start.3 = (bf16[1072,1024]{1,0:T(8,128)(2,1)S(1)}, bf16[1072,1024]{1,0:T(8,128)(2,1)}, u32[]{:S(2)}) copy-start(bf16[1072,1024]{1,0:T(8,128)(2,1)} %get-tuple-element.19) | copy-start | bytes 6586372
  76.4 73.2 %all-to-all-start = ((bf16[64,15,1024]{2,1,0:T(8,128)(2,1)}), bf16[64,15,1024]{2,1,0:T(8,128)(2,1)}, u32[]{:S(2)}, u32[]{:S(2)}) async-start(bf16[64,15,1024]{2,1,0:T(8,128)(2,1)} %reshape.201), calls=%async_computation | async-start | bytes 4194304 | tf_op jit(solution)/shard_map/all_to_all | solution.py:98
  149.6 112.5 %all-to-all-start.3 = ((bf16[64,15,1024]{2,1,0:T(8,128)(2,1)}), bf16[64,15,1024]{2,1,0:T(8,128)(2,1)}, u32[]{:S(2)}, u32[]{:S(2)}) async-start(bf16[64,15,1024]{2,1,0:T(8,128)(2,1)} %reshape.211), calls=%async_computation.3 | async-start | bytes 4194304 | tf_op jit(solution)/shard_map/all_to_all | solution.py:99
  159.0 499.9 %all-gather.11.cloned.1.call-start = ((), (), s32[]{:S(2)}) async-start(), calls=%async_computation.7 | async-start | bytes 6389760 | tf_op jit(solution)/shard_map/all_gather | solution.py:10
  250.4 3.0 copy-start.6
  253.5 1.2 copy-start.18
  253.5 2.4 copy-start.8
  254.7 1.2 copy-start.20
  262.1 68.5 %all-to-all-start.1 = ((bf16[64,15,1024]{2,1,0:T(8,128)(2,1)}), bf16[64,15,1024]{2,1,0:T(8,128)(2,1)}, u32[]{:S(2)}, u32[]{:S(2)}) async-start(bf16[64,15,1024]{2,1,0:T(8,128)(2,1)} %reshape_transpose_reshape.8), calls=%async_computation.1 | async-start | bytes 4194304 | tf_op jit(solution)/shard_map/all_to_all | solution.py:139
  277.3 3.1 copy-start.7
  277.3 3.1 copy-start.19
  277.3 3.1 copy-start.21
  330.6 61.3 %all-to-all-start.4 = ((bf16[64,15,1024]{2,1,0:T(8,128)(2,1)}), bf16[64,15,1024]{2,1,0:T(8,128)(2,1)}, u32[]{:S(2)}, u32[]{:S(2)}) async-start(bf16[64,15,1024]{2,1,0:T(8,128)(2,1)} %reshape_transpose_reshape.9), calls=%async_computation.4 | async-start | bytes 4194304 | tf_op jit(solution)/shard_map/all_to_all | solution.py:146
  662.7 27.4 %copy-start.15 = (bf16[112,1024]{1,0:T(8,128)(2,1)S(1)}, bf16[112,1024]{1,0:T(8,128)(2,1)}, u32[]{:S(2)}) copy-start(bf16[112,1024]{1,0:T(8,128)(2,1)} %slice.58) | copy-start | bytes 688132
  690.1 1.1 copy-start.9
  690.1 1.2 copy-start.14
  693.1 1.6 copy-start.5
  700.2 3.0 copy-start.4
  700.2 3.0 copy-start.13
Sparse Core Ops, SparseCore 0:
  32.5 116.2 all-gather.12
  152.1 89.3 all-gather.14
  244.8 99.2 all-gather.16
  347.3 87.9 all-gather.6
  438.4 83.2 all-gather.8
  524.9 83.0 all-gather.10
